TPU v7x, 32 devices: a whole 2x2x4 slice. The times are simulated.
32 devices in a mesh: seq: 8 (over z, x), tensor: 4 (over y, core).
Axes of the slice: x: 2, y: 2, z: 4, core: 2. Of those that a mesh axis runs over, the one named last changes fastest.
Arguments:
- tokens: bfloat16 [8192, 1024], P('seq'), may hold values from -6 to 6
- item_ids: int32 [8192], replicated, may hold values from 0 to 8, as said below
- text_states: bfloat16 [9, 128, 1024], replicated, may hold values from -6 to 6
- text_lengths: int32 [9], replicated, may hold values from 8 to 128
- norm_gain: bfloat16 [3, 1024], replicated, may hold values from 0.25 to 1.75
- norm_shift: bfloat16 [3, 1024], replicated, may hold values from -3 to 3
- w_self: bfloat16 [3, 1024, 1024], P(None, None, 'tensor'), may hold values from -0.1875 to 0.1875
- b_self: bfloat16 [2, 1024], P(None, 'tensor'), may hold values from -3 to 3
- w_self_out: bfloat16 [1024, 1024], P('tensor'), may hold values from -1 to 1
- w_cross_q: bfloat16 [1024, 1024], P(None, 'tensor'), may hold values from -0.1875 to 0.1875
- w_cross_kv: bfloat16 [2, 1024, 1024], P(None, None, 'tensor'), may hold values from -0.1875 to 0.1875
- b_cross: bfloat16 [2, 1024], P(None, 'tensor'), may hold values from -3 to 3
- w_cross_out: bfloat16 [1024, 1024], P('tensor'), may hold values from -0.75 to 0.75
- w_up: bfloat16 [1024, 4096], P(None, 'tensor'), may hold values from -0.1875 to 0.1875
- b_up: bfloat16 [4096], P('tensor'), may hold values from -3 to 3
- w_down: bfloat16 [4096, 1024], P('tensor'), may hold values from -0.09375 to 0.09375
- out_bias: bfloat16 [3, 1024], replicated, may hold values from -3 to 3
- d_out: bfloat16 [8192, 1024], P('seq'), may hold values from -6 to 6
Outputs:
- out: bfloat16 [8192, 1024], P('seq')
- grad_tokens: float32 [8192, 1024], P('seq')
- grad_text_states: float32 [9, 128, 1024], replicated
- grad_norm_gain: float32 [3, 1024], P(None, 'tensor')
- grad_norm_shift: float32 [3, 1024], P(None, 'tensor')
- grad_w_self: float32 [3, 1024, 1024], P(None, None, 'tensor')
- grad_b_self: float32 [2, 1024], P(None, 'tensor')
- grad_w_self_out: float32 [1024, 1024], P('tensor')
- grad_w_cross_q: float32 [1024, 1024], P(None, 'tensor')
- grad_w_cross_kv: float32 [2, 1024, 1024], P(None, None, 'tensor')
- grad_b_cross: float32 [2, 1024], P(None, 'tensor')
- grad_w_cross_out: float32 [1024, 1024], P('tensor')
- grad_w_up: float32 [1024, 4096], P(None, 'tensor')
- grad_b_up: float32 [4096], P('tensor')
- grad_w_down: float32 [4096, 1024], P('tensor')
- grad_out_bias: float32 [3, 1024], P(None, 'tensor')
Inputs may be any that keep to these rules, and one draw needn't show every extreme that they name: `item_ids`: item ids never fall along the tokens and each of 0 to 8 occurs; every item but the first and the last holds exactly 1024 tokens, and the first and the last together hold 1024.
All inputs are finite; a program needn't handle non-finite values.
Results may differ from a plain program's by a relative error of at most 0.035.
Values may be sent and summed in bfloat16 or wider, within the bound.
No kernel may reach another device: no remote copies, remote signals or barrier semaphores. Data moves between devices by JAX's collectives and lax.ppermute only.
A program may use at most 256 MiB of HBM per device.

v0:
```python
import jax
import jax.numpy as jnp
from jax import lax
from jax.sharding import PartitionSpec as P

HEAD_SIZE = 64
ITEM_LEN = 1024


epsilon = 1e-05
masked_fill = -1e30


def shifted(value, axis, steps):
    count = lax.axis_size(axis)
    leading, last = (max(0, -steps), min(count, count - steps))
    return lax.ppermute(value, axis, [(source, source + steps) for source in range(leading, last)])


def matmul_low(left, right):
    return jnp.dot(left, right, preferred_element_type=jnp.float32)


def contract_rows(left, right):
    return jnp.einsum("ra,rb->ab", left, right, preferred_element_type=jnp.float32)


def times_transpose(left, right):
    return jnp.einsum("ra,ba->rb", left, right, preferred_element_type=jnp.float32)


def layer_norm(rows_in, gain, shift):
    row_mean = jnp.mean(rows_in, axis=-1, keepdims=True)
    centered = rows_in - row_mean
    variance = jnp.mean(centered * centered, axis=-1, keepdims=True)
    inv_scale = lax.rsqrt(variance + epsilon)
    normal = centered * inv_scale
    return (normal * gain + shift, normal, inv_scale)


def norm_back(grad_normed, normal, inv_scale, gain):
    grad_normal = grad_normed * gain
    grad_mean = jnp.mean(grad_normal, axis=-1, keepdims=True)
    proj_mean = jnp.mean(grad_normal * normal, axis=-1, keepdims=True)
    return inv_scale * (grad_normal - grad_mean - normal * proj_mean)


def split_heads(matrix, head_size):
    return matrix.reshape(matrix.shape[0], matrix.shape[1] // head_size, head_size)


def per_device(
    tokens,
    item_ids,
    text_states,
    text_lengths,
    norm_gain,
    norm_shift,
    w_self,
    b_self,
    w_self_out,
    w_cross_q,
    w_cross_kv,
    b_cross,
    w_cross_out,
    w_up,
    b_up,
    w_down,
    out_bias,
    d_out,
):
    row_count = tokens.shape[0]
    local_width = w_self.shape[2]
    head_count = local_width // HEAD_SIZE
    score_scale = HEAD_SIZE ** (-0.5)
    seq_rank = lax.axis_index("seq")
    tensor_rank = lax.axis_index("tensor")
    first_row = seq_rank * row_count
    row_pos = first_row + jnp.arange(row_count, dtype=jnp.int32)
    local_ids = lax.dynamic_slice_in_dim(item_ids, first_row, row_count)

    def tensor_rows(partial_rows):
        return lax.psum(partial_rows.astype(jnp.bfloat16), "tensor").astype(jnp.float32)

    def tensor_grads(partial_rows):
        return lax.psum(partial_rows.astype(jnp.bfloat16), "tensor").astype(jnp.float32)

    def block_mask(block_start):
        key_pos = block_start + jnp.arange(row_count, dtype=jnp.int32)
        key_ids = lax.dynamic_slice_in_dim(item_ids, jnp.maximum(block_start, 0), row_count)
        return (
            (key_pos[None, :] >= 0)
            & (key_pos[None, :] <= row_pos[:, None])
            & (key_ids[None, :] == local_ids[:, None])
        )

    def block_live(block_start):
        last_key = lax.dynamic_index_in_dim(
            item_ids, jnp.maximum(block_start + row_count - 1, 0), keepdims=False
        )
        return (block_start >= 0) & (last_key == local_ids[0])

    residual = tokens.astype(jnp.float32)
    gain_rows = norm_gain.astype(jnp.float32)
    shift_rows = norm_shift.astype(jnp.float32)
    bias_rows = out_bias.astype(jnp.float32)
    normed_one, normal_one, inv_one = layer_norm(residual, gain_rows[0], shift_rows[0])
    inputs_one = normed_one.astype(jnp.bfloat16)
    queries = (matmul_low(inputs_one, w_self[0]) + b_self[0].astype(jnp.float32)).astype(
        jnp.bfloat16
    )
    keys_local = matmul_low(inputs_one, w_self[1]).astype(jnp.bfloat16)
    values_local = (matmul_low(inputs_one, w_self[2]) + b_self[1].astype(jnp.float32)).astype(
        jnp.bfloat16
    )
    query_heads = split_heads(queries, HEAD_SIZE)

    def scores_of(key_block, block_start):
        key_heads = split_heads(key_block, HEAD_SIZE)
        scores = score_scale * jnp.einsum(
            "qhd,khd->hqk", query_heads, key_heads, preferred_element_type=jnp.float32
        )
        return (scores, block_mask(block_start)[None])

    def attend_block(state_now, key_block, value_block, block_start):
        old_max, old_total, old_acc = state_now
        scores, allowed = scores_of(key_block, block_start)
        new_max = jnp.maximum(old_max, jnp.max(jnp.where(allowed, scores, masked_fill), axis=-1))
        weights = jnp.where(allowed, jnp.exp(scores - new_max[..., None]), 0.0)
        factor = jnp.exp(old_max - new_max)
        new_total = old_total * factor + jnp.sum(weights, axis=-1)
        update = jnp.einsum(
            "hqk,khd->hqd",
            weights.astype(jnp.bfloat16),
            split_heads(value_block, HEAD_SIZE),
            preferred_element_type=jnp.float32,
        )
        return (new_max, new_total, old_acc * factor[..., None] + update)

    moving = (keys_local, values_local)
    moving = shifted((moving[0], moving[1]), "seq", 1)
    received = [moving]
    start_max = jnp.full((head_count, row_count), masked_fill, jnp.float32)
    start_total = jnp.zeros((head_count, row_count), jnp.float32)
    start_acc = jnp.zeros((head_count, row_count, HEAD_SIZE), jnp.float32)
    attn_state = attend_block(
        (start_max, start_total, start_acc), keys_local, values_local, first_row
    )
    back_index = 1
    block_start = first_row - back_index * row_count
    key_block, value_block = received[back_index - 1]

    def attend_far(state_in, key_block=key_block, value_block=value_block, block_start=block_start):
        return attend_block(state_in, key_block, value_block, block_start)

    def keep_state(state_in):
        return state_in

    attn_state = lax.cond(block_live(block_start), attend_far, keep_state, attn_state)
    run_max, run_total, run_acc = attn_state
    attn_heads = run_acc / run_total[..., None]
    log_total = run_max + jnp.log(run_total)
    attended = (
        jnp.transpose(attn_heads, (1, 0, 2)).reshape(row_count, local_width).astype(jnp.bfloat16)
    )
    after_self = residual + (tensor_rows(matmul_low(attended, w_self_out)) + bias_rows[0])
    normed_two, normal_two, inv_two = layer_norm(after_self, gain_rows[1], shift_rows[1])
    inputs_two = normed_two.astype(jnp.bfloat16)
    cross_queries = (matmul_low(inputs_two, w_cross_q) + b_cross[0].astype(jnp.float32)).astype(
        jnp.bfloat16
    )
    item_total = text_states.shape[0]
    slot_count = text_states.shape[1]
    slot_total = item_total * slot_count
    local_items = min(item_total, (row_count + ITEM_LEN - 2) // ITEM_LEN + 1)
    window_slots = local_items * slot_count
    start_item = jnp.minimum(local_ids[0], item_total - local_items)
    text_flat = text_states.reshape(slot_total, text_states.shape[2])
    text_window = lax.dynamic_slice_in_dim(text_states, start_item, local_items, 0).reshape(
        window_slots, text_states.shape[2]
    )
    text_keys = matmul_low(text_window, w_cross_kv[0]).astype(jnp.bfloat16)
    text_values = (matmul_low(text_window, w_cross_kv[1]) + b_cross[1].astype(jnp.float32)).astype(
        jnp.bfloat16
    )
    window_index = jnp.arange(window_slots, dtype=jnp.int32)
    slot_item = start_item + window_index // slot_count
    item_index = jnp.arange(item_total, dtype=jnp.int32)
    slot_length = jnp.sum(
        jnp.where(slot_item[:, None] == item_index[None, :], text_lengths[None, :], 0), axis=1
    )
    slot_live = window_index % slot_count < slot_length
    cross_allowed = ((slot_item[None, :] == local_ids[:, None]) & slot_live[None, :])[None]
    cross_heads = split_heads(cross_queries, HEAD_SIZE)
    text_key_heads = split_heads(text_keys, HEAD_SIZE)
    text_value_heads = split_heads(text_values, HEAD_SIZE)
    cross_scores = score_scale * jnp.einsum(
        "qhd,shd->hqs", cross_heads, text_key_heads, preferred_element_type=jnp.float32
    )
    cross_filled = jnp.where(cross_allowed, cross_scores, masked_fill)
    cross_exp = jnp.exp(cross_filled - jnp.max(cross_filled, axis=-1, keepdims=True))
    cross_probs = cross_exp / jnp.sum(cross_exp, axis=-1, keepdims=True)
    cross_low = cross_probs.astype(jnp.bfloat16)
    cross_rows = jnp.einsum(
        "hqs,shd->qhd", cross_low, text_value_heads, preferred_element_type=jnp.float32
    )
    cross_attended = cross_rows.reshape(row_count, local_width).astype(jnp.bfloat16)
    after_cross = after_self + (tensor_rows(matmul_low(cross_attended, w_cross_out)) + bias_rows[1])
    normed_three, normal_three, inv_three = layer_norm(after_cross, gain_rows[2], shift_rows[2])
    inputs_three = normed_three.astype(jnp.bfloat16)
    hidden_pre = matmul_low(inputs_three, w_up) + b_up.astype(jnp.float32)
    hidden_act, gelu_back = jax.vjp(jax.nn.gelu, hidden_pre)
    hidden_low = hidden_act.astype(jnp.bfloat16)
    output_rows = after_cross + (tensor_rows(matmul_low(hidden_low, w_down)) + bias_rows[2])
    grad_final = d_out.astype(jnp.float32)
    grad_low = grad_final.astype(jnp.bfloat16)
    grad_bias_three = jnp.sum(grad_low.astype(jnp.float32), axis=0)
    grad_w_down = contract_rows(hidden_low, grad_low)
    grad_hidden = times_transpose(grad_low, w_down)
    grad_pre = gelu_back(grad_hidden)[0].astype(jnp.bfloat16)
    grad_b_up = jnp.sum(grad_pre.astype(jnp.float32), axis=0)
    grad_w_up = contract_rows(inputs_three, grad_pre)
    grad_normed_three = tensor_grads(times_transpose(grad_pre, w_up))
    grad_gain_three = jnp.sum(grad_normed_three * normal_three, axis=0)
    grad_shift_three = jnp.sum(grad_normed_three, axis=0)
    grad_after_cross = grad_final + norm_back(
        grad_normed_three, normal_three, inv_three, gain_rows[2]
    )
    grad_cross_low = grad_after_cross.astype(jnp.bfloat16)
    grad_bias_two = jnp.sum(grad_cross_low.astype(jnp.float32), axis=0)
    grad_w_cross_out = contract_rows(cross_attended, grad_cross_low)
    grad_cross_att = times_transpose(grad_cross_low, w_cross_out).astype(jnp.bfloat16)
    grad_cross_heads = split_heads(grad_cross_att, HEAD_SIZE)
    grad_cross_probs = jnp.einsum(
        "qhd,shd->hqs", grad_cross_heads, text_value_heads, preferred_element_type=jnp.float32
    )
    cross_inner = jnp.sum(cross_probs * grad_cross_probs, axis=-1, keepdims=True)
    grad_cross_scores = (cross_probs * (grad_cross_probs - cross_inner)).astype(jnp.bfloat16)
    grad_cross_q = (
        (
            score_scale
            * jnp.einsum(
                "hqs,shd->qhd",
                grad_cross_scores,
                text_key_heads,
                preferred_element_type=jnp.float32,
            )
        )
        .reshape(row_count, local_width)
        .astype(jnp.bfloat16)
    )
    key_window_part = (
        score_scale
        * jnp.einsum(
            "hqs,qhd->shd", grad_cross_scores, cross_heads, preferred_element_type=jnp.float32
        )
    ).reshape(window_slots, local_width)
    value_window_part = jnp.einsum(
        "hqs,qhd->shd", cross_low, grad_cross_heads, preferred_element_type=jnp.float32
    ).reshape(window_slots, local_width)
    empty_slots = jnp.zeros((slot_total, local_width), jnp.float32)
    text_key_part = lax.dynamic_update_slice_in_dim(
        empty_slots, key_window_part, start_item * slot_count, 0
    )
    text_value_part = lax.dynamic_update_slice_in_dim(
        empty_slots, value_window_part, start_item * slot_count, 0
    )
    text_key_sum, text_value_sum = (
        lax.psum(text_key_part.astype(jnp.bfloat16), "seq").astype(jnp.float32),
        lax.psum(text_value_part.astype(jnp.bfloat16), "seq").astype(jnp.float32),
    )
    grad_text_keys = text_key_sum.astype(jnp.bfloat16)
    grad_text_values = text_value_sum.astype(jnp.bfloat16)
    grad_w_cross_kv = jnp.stack(
        (contract_rows(text_flat, grad_text_keys), contract_rows(text_flat, grad_text_values))
    )
    grad_text_part = times_transpose(grad_text_keys, w_cross_kv[0]) + times_transpose(
        grad_text_values, w_cross_kv[1]
    )
    grad_text = (
        lax.psum(grad_text_part.astype(jnp.bfloat16), "tensor")
        .astype(jnp.float32)
        .reshape(text_states.shape)
    )
    grad_query_bias = jnp.sum(grad_cross_q.astype(jnp.float32), axis=0)
    grad_value_bias = jnp.sum(grad_text_values.astype(jnp.float32), axis=0)
    grad_w_cross_q = contract_rows(inputs_two, grad_cross_q)
    grad_normed_two = tensor_grads(times_transpose(grad_cross_q, w_cross_q))
    grad_gain_two = jnp.sum(grad_normed_two * normal_two, axis=0)
    grad_shift_two = jnp.sum(grad_normed_two, axis=0)
    grad_after_self = grad_after_cross + norm_back(
        grad_normed_two, normal_two, inv_two, gain_rows[1]
    )
    grad_self_low = grad_after_self.astype(jnp.bfloat16)
    grad_bias_one = jnp.sum(grad_self_low.astype(jnp.float32), axis=0)
    grad_w_self_out = contract_rows(attended, grad_self_low)
    grad_attn_rows = times_transpose(grad_self_low, w_self_out).astype(jnp.bfloat16)
    grad_attn_heads = split_heads(grad_attn_rows, HEAD_SIZE)
    row_inner = jnp.einsum("qhd,hqd->hq", grad_attn_heads.astype(jnp.float32), attn_heads)

    def back_block(grad_q_in, key_block, value_block, block_start):
        scores, allowed = scores_of(key_block, block_start)
        attn_probs = jnp.where(allowed, jnp.exp(scores - log_total[..., None]), 0.0)
        key_heads = split_heads(key_block, HEAD_SIZE)
        value_heads = split_heads(value_block, HEAD_SIZE)
        grad_probs = jnp.einsum(
            "qhd,khd->hqk", grad_attn_heads, value_heads, preferred_element_type=jnp.float32
        )
        grad_scores = (attn_probs * (grad_probs - row_inner[..., None])).astype(jnp.bfloat16)
        grad_q_out = grad_q_in + score_scale * jnp.einsum(
            "hqk,khd->qhd", grad_scores, key_heads, preferred_element_type=jnp.float32
        )
        grad_key_block = score_scale * jnp.einsum(
            "hqk,qhd->khd", grad_scores, query_heads, preferred_element_type=jnp.float32
        )
        grad_value_block = jnp.einsum(
            "hqk,qhd->khd",
            attn_probs.astype(jnp.bfloat16),
            grad_attn_heads,
            preferred_element_type=jnp.float32,
        )
        return (
            grad_q_out,
            grad_key_block.reshape(row_count, local_width),
            grad_value_block.reshape(row_count, local_width),
        )

    moving = (keys_local, values_local)
    moving = shifted((moving[0], moving[1]), "seq", 1)
    again = [moving]
    start_grad_q = jnp.zeros((row_count, head_count, HEAD_SIZE), jnp.float32)
    grad_q, grad_keys_own, grad_values_own = back_block(
        start_grad_q, keys_local, values_local, first_row
    )
    back_index = 1
    block_start = first_row - back_index * row_count
    key_block, value_block = again[back_index - 1]

    def back_far(grad_q_in, key_block=key_block, value_block=value_block, block_start=block_start):
        return back_block(grad_q_in, key_block, value_block, block_start)

    def skip_far(grad_q_in):
        zero_block = jnp.zeros((row_count, local_width), jnp.float32)
        return (grad_q_in, zero_block, zero_block)

    grad_q, grad_key_far, grad_value_far = lax.cond(
        block_live(block_start), back_far, skip_far, grad_q
    )
    far_grads = [(grad_key_far, grad_value_far)]
    back_index = 1
    grad_key_far, grad_value_far = far_grads[back_index - 1]
    carry_keys = shifted(grad_key_far.astype(jnp.bfloat16), "seq", -1).astype(grad_key_far.dtype)
    carry_values = shifted(grad_value_far.astype(jnp.bfloat16), "seq", -1).astype(
        grad_value_far.dtype
    )
    grad_keys = grad_keys_own + carry_keys
    grad_values = grad_values_own + carry_values
    grad_queries = grad_q.reshape(row_count, local_width).astype(jnp.bfloat16)
    grad_keys_low = grad_keys.astype(jnp.bfloat16)
    grad_values_low = grad_values.astype(jnp.bfloat16)
    grad_w_self = jnp.stack(
        (
            contract_rows(inputs_one, grad_queries),
            contract_rows(inputs_one, grad_keys_low),
            contract_rows(inputs_one, grad_values_low),
        )
    )
    grad_b_self = jnp.stack(
        (
            jnp.sum(grad_queries.astype(jnp.float32), axis=0),
            jnp.sum(grad_values_low.astype(jnp.float32), axis=0),
        )
    )
    grad_normed_one = tensor_grads(
        times_transpose(grad_queries, w_self[0])
        + times_transpose(grad_keys_low, w_self[1])
        + times_transpose(grad_values_low, w_self[2])
    )
    grad_gain_one = jnp.sum(grad_normed_one * normal_one, axis=0)
    grad_shift_one = jnp.sum(grad_normed_one, axis=0)
    grad_tokens = grad_after_self + norm_back(grad_normed_one, normal_one, inv_one, gain_rows[0])

    def local_cols(full_rows):
        return lax.dynamic_slice_in_dim(full_rows, tensor_rank * local_width, local_width, axis=1)

    grad_gain = local_cols(jnp.stack((grad_gain_one, grad_gain_two, grad_gain_three)))
    grad_shift = local_cols(jnp.stack((grad_shift_one, grad_shift_two, grad_shift_three)))
    grad_bias_out = local_cols(jnp.stack((grad_bias_one, grad_bias_two, grad_bias_three)))
    summed = (
        lax.psum(grad_gain.astype(jnp.bfloat16), "seq").astype(jnp.float32),
        lax.psum(grad_shift.astype(jnp.bfloat16), "seq").astype(jnp.float32),
        lax.psum(grad_w_self.astype(jnp.bfloat16), "seq").astype(jnp.float32),
        lax.psum(grad_b_self.astype(jnp.bfloat16), "seq").astype(jnp.float32),
        lax.psum(grad_w_self_out.astype(jnp.bfloat16), "seq").astype(jnp.float32),
        lax.psum(grad_w_cross_q.astype(jnp.bfloat16), "seq").astype(jnp.float32),
        lax.psum(grad_query_bias.astype(jnp.bfloat16), "seq").astype(jnp.float32),
        lax.psum(grad_w_cross_out.astype(jnp.bfloat16), "seq").astype(jnp.float32),
        lax.psum(grad_w_up.astype(jnp.bfloat16), "seq").astype(jnp.float32),
        lax.psum(grad_b_up.astype(jnp.bfloat16), "seq").astype(jnp.float32),
        lax.psum(grad_w_down.astype(jnp.bfloat16), "seq").astype(jnp.float32),
        lax.psum(grad_bias_out.astype(jnp.bfloat16), "seq").astype(jnp.float32),
    )
    grad_b_cross = jnp.stack((summed[6], grad_value_bias))
    return (
        output_rows.astype(jnp.bfloat16),
        grad_tokens,
        grad_text,
        summed[0],
        summed[1],
        summed[2],
        summed[3],
        summed[4],
        summed[5],
        grad_w_cross_kv,
        grad_b_cross,
        summed[7],
        summed[8],
        summed[9],
        summed[10],
        summed[11],
    )


def solution(mesh):
    placed = (
        P("seq", None),
        P(),
        P(),
        P(),
        P(),
        P(),
        P(None, None, "tensor"),
        P(None, "tensor"),
        P("tensor", None),
        P(None, "tensor"),
        P(None, None, "tensor"),
        P(None, "tensor"),
        P("tensor", None),
        P(None, "tensor"),
        P("tensor"),
        P("tensor", None),
        P(),
        P("seq", None),
    )
    return jax.shard_map(
        per_device,
        mesh=mesh,
        in_specs=placed,
        out_specs=(
            P("seq", None),
            P("seq", None),
            P(),
            P(None, "tensor"),
            P(None, "tensor"),
            P(None, None, "tensor"),
            P(None, "tensor"),
            P("tensor", None),
            P(None, "tensor"),
            P(None, None, "tensor"),
            P(None, "tensor"),
            P("tensor", None),
            P(None, "tensor"),
            P("tensor"),
            P("tensor", None),
            P(None, "tensor"),
        ),
        check_vma=False,
    )
```

profile of v0, /device:TPU:0, one launch (start us, length us, event | category | flops | bytes accessed | tf_op | source)
XLA Modules:
  0.0 914.3 jit_solution(16476937947176585763)
XLA Ops:
  14.3 4.9 collective-permute-start
  32.1 4.4 select_reduce_fusion.1
  42.3 10.6 %fusion.71 = f32[4,1024,64]{1,2,0:T(8,128)} fusion(bf16[1024,4,64]{0,2,1:T(8,128)(2,1)} %bitcast.18, f32[4,1024,1024]{1,2,0:T(8,128)} %copy-done.5, f32[4,1024]{1,0:T(4,128)S(1)} %broadcast_maximum_fusion, pred[1024,1024]{0,1:T(8,128)(4,1)} %copy-done.18, f32[4,1024]{1,0:T(4,128)S(1)} %get-tuple-element.219), kind=kOutput, calls=%fused_computation.135 | convolution fusion | flops 553910272 | bytes 19431424 | tf_op jit(solution)/shard_map/hqk,khd->hqd/dot_general | solution.py:132
  64.6 59.1 %all-reduce.10.cloned.1.call-done = bf16[1024,1024]{1,0:T(8,128)(2,1)} async-done(((bf16[1024,1024]{1,0:T(8,128)(2,1)}), bf16[1024,1024]{1,0:T(8,128)(2,1)}) %all-reduce.10.cloned.1.call-update) | async-done | bytes 2097168 | tf_op jit(solution)/shard_map/psum | solution.py:83
  132.6 4.9 fusion.151
  143.7 51.0 %all-reduce.12.cloned.1.call-done = bf16[1024,1024]{1,0:T(8,128)(2,1)} async-done(((bf16[1024,1024]{1,0:T(8,128)(2,1)}), bf16[1024,1024]{1,0:T(8,128)(2,1)}) %all-reduce.12.cloned.1.call-update) | async-done | bytes 2097168 | tf_op jit(solution)/shard_map/psum | solution.py:83
  204.4 5.7 fusion.141
  215.4 7.0 convolution_convert_fusion.1
  226.8 40.0 %all-reduce.14.cloned.1.call-done = bf16[1024,1024]{1,0:T(8,128)(2,1)} async-done(((bf16[1024,1024]{1,0:T(8,128)(2,1)}), bf16[1024,1024]{1,0:T(8,128)(2,1)}) %all-reduce.14.cloned.1.call-update) | async-done | bytes 2097168 | tf_op jit(solution)/shard_map/psum | solution.py:86
  266.8 5.1 fusion.62
  298.2 41.3 %all-reduce.16.cloned.1.call-done = bf16[1024,1024]{1,0:T(8,128)(2,1)} async-done(((bf16[1024,1024]{1,0:T(8,128)(2,1)}), bf16[1024,1024]{1,0:T(8,128)(2,1)}) %all-reduce.16.cloned.1.call-update) | async-done | bytes 2097168 | tf_op jit(solution)/shard_map/psum | solution.py:86
  339.4 5.0 fusion.63
  344.5 4.4 convert_reduce_fusion.6
  354.2 10.5 %fusion.22 = f32[4,64,1024]{2,1,0:T(8,128)} fusion(bf16[1024,4,64]{0,2,1:T(8,128)(2,1)} %bitcast.42, f32[4,1024,1024]{1,2,0:T(8,128)} %copy-done.5, f32[4,1024]{1,0:T(4,128)S(1)} %log_add_fusion, pred[1024,1024]{0,1:T(8,128)(4,1)S(1)} %copy-done.19), kind=kOutput, calls=%fused_computation.36 | convolution fusion | flops 553648128 | bytes 19415040 | tf_op jit(solution)/shard_map/hqk,qhd->khd/dot_general | solution.py:316
  364.7 9.3 %multiply_convert_fusion.1 = bf16[4,1024,1024]{1,2,0:T(8,128)(2,1)S(1)} fusion(f32[4,1024,1024]{1,2,0:T(8,128)} %copy-done.5, bf16[1024,4,64]{0,2,1:T(8,128)(2,1)} %bitcast.42, bf16[1024,4,64]{0,2,1:T(8,128)(2,1)} %bitcast.18, f32[4,1024]{1,0:T(4,128)S(1)} %get-tuple-element.240, f32[4,1024]{1,0:T(4,128)S(1)} %log_add_fusion, ...), kind=kOutput, calls=%fused_computation.29 | convolution fusion | flops 562036736 | bytes 27295744 | tf_op jit(solution)/shard_map/qhd,khd->hqk/dot_general | solution.py:306
  378.0 5.8 conditional.3
  390.9 6.0 convolution_multiply_fusion.2
  396.9 34.0 %collective-permute-done.2 = bf16[1024,256]{0,1:T(8,128)(2,1)S(1)} collective-permute-done((bf16[1024,256]{0,1:T(8,128)(2,1)}, bf16[1024,256]{0,1:T(8,128)(2,1)S(1)}, u32[]{:S(2)}, u32[]{:S(2)}) %collective-permute-start.2) | collective-permute-done | bytes 524320 | tf_op jit(solution)/shard_map/ppermute | solution.py:17
  431.9 9.4 %collective-permute-done.3 = bf16[1024,256]{0,1:T(8,128)(2,1)S(1)} collective-permute-done((bf16[1024,256]{0,1:T(8,128)(2,1)}, bf16[1024,256]{0,1:T(8,128)(2,1)S(1)}, u32[]{:S(2)}, u32[]{:S(2)}) %collective-permute-start.3) | collective-permute-done | bytes 524320 | tf_op jit(solution)/shard_map/ppermute | solution.py:17
  444.7 7.1 convolution_convert_fusion.4
  455.8 267.6 %all-reduce.18.cloned.1.call-done = (bf16[1152,256]{0,1:T(8,128)(2,1)}, bf16[1152,256]{0,1:T(8,128)(2,1)}, bf16[3,1024,256]{2,1,0:T(8,128)(2,1)}, bf16[256,1024]...) async-done(((bf16[1152,256]{0,1:T(8,128)(2,1)}, ...) | async-done | bytes 8519696 | tf_op jit(solution)/shard_map/psum | solution.py:269
  754.5 96.6 %all-reduce.20.cloned.1.call-done = (bf16[1024,1024]{1,0:T(8,128)(2,1)}, bf16[1024,1024]{1,0:T(8,128)(2,1)}, bf16[9,128,1024]{2,1,0:T(8,128)(2,1)}) async-done(((bf16[1024,1024]{1,0:T(8,128)(2,1)}, bf16[1024,1024]{1,0:T(8,128)(2,1)}, bf16[9,128,1024]{2,1,0:T(8,128)(2,1)}), (bf16[1024,1024]{1,0:T(8,128)(2,1)}, bf16[1024,1024]{1,0:T(8,128)(2,1)}, ...) | async-done | bytes 6553616 | tf_op jit(solution)/shard_map/psum | solution.py:83
  854.9 37.5 %all-reduce = (bf16[3,256]{1,0:T(4,128)(2,1)S(1)}, bf16[3,256]{1,0:T(4,128)(2,1)S(1)}, bf16[2,256]{1,0:T(2,128)(2,1)S(1)}, bf16[1,256]{1,0:T(2,128)(2,1)S(1)}, b...) all-reduce(bf16[3,256]{1,0:T(4,128)(2,1)S(1)} %fusion.121, ...), channel_id=1, replica_groups=mesh['seq'=8,'tensor'=4] {'seq'}, use_global_device_ids=true, to_apply=%region_36.37 | all-reduce | flops 4096 | bytes 16384 | tf_op jit(solution)/shard_map/psum | solution.py:390
  895.4 4.4 reshape.525
  (290 shorter events, 166.9 us)
Async XLA Ops:
  7.2 51.7 %copy-start = (bf16[9,128,1024]{2,1,0:T(8,128)(2,1)S(1)}, bf16[9,128,1024]{2,1,0:T(8,128)(2,1)}, u32[]{:S(2)}) copy-start(bf16[9,128,1024]{2,1,0:T(8,128)(2,1)} %param.24) | copy-start | bytes 7077892
  7.2 116.4 %all-reduce.10.cloned.1.call-start = ((), (), s32[]{:S(2)}) async-start(), calls=%async_computation | async-start | bytes 4194304 | tf_op jit(solution)/shard_map/psum | solution.py:83
  12.7 12.4 %copy-start.65 = (s32[8192]{0:T(1024)S(1)}, s32[8192]{0:T(1024)}, u32[]{:S(2)}) copy-start(s32[8192]{0:T(1024)} %param.23) | copy-start | bytes 98308
  14.3 38.7 %collective-permute-start = (bf16[1024,256]{0,1:T(8,128)(2,1)}, bf16[1024,256]{0,1:T(8,128)(2,1)S(1)}, u32[]{:S(2)}, u32[]{:S(2)}) collective-permute-start(bf16[1024,256]{0,1:T(8,128)(2,1)} %convolution_convert_fusion.15), channel_id=1, source_target_pairs={{0,4},{4,8},{8,12},{12,16},{16,20},{20,24},{24,28},{1,5},{5,9},{9,... | collective-permute-start | bytes 1572872 | tf_op jit(solution)/shard_map/ppermute | solution.py:17
  20.8 32.2 %collective-permute-start.1 = (bf16[1024,256]{0,1:T(8,128)(2,1)}, bf16[1024,256]{0,1:T(8,128)(2,1)}, u32[]{:S(2)}, u32[]{:S(2)}) collective-permute-start(bf16[1024,256]{0,1:T(8,128)(2,1)} %fusion.76), channel_id=1, source_target_pairs={{0,4},{4,8},{8,12},{12,16},{16,20},{20,24},{24,28},{1,5},{5,9},{9,... | collective-permute-start | bytes 1572872 | tf_op jit(solution)/shard_map/ppermute | solution.py:17
  58.5 136.2 %all-reduce.12.cloned.1.call-start = ((), (), s32[]{:S(2)}) async-start(), calls=%async_computation.1 | async-start | bytes 4194304 | tf_op jit(solution)/shard_map/psum | solution.py:83
  143.2 123.6 %all-reduce.14.cloned.1.call-start = ((), (), s32[]{:S(2)}) async-start(), calls=%async_computation.2 | async-start | bytes 4194304 | tf_op jit(solution)/shard_map/psum | solution.py:86
  143.7 78.8 %copy-start.68 = (f32[1024]{0:T(1024)}, f32[1024]{0:T(1024)S(1)}, u32[]{:S(2)}) copy-start(f32[1024]{0:T(1024)S(1)} %convert_element_type.316) | copy-start | bytes 12292
  215.2 124.3 %all-reduce.16.cloned.1.call-start = ((), (), s32[]{:S(2)}) async-start(), calls=%async_computation.3 | async-start | bytes 4194304 | tf_op jit(solution)/shard_map/psum | solution.py:86
  287.8 435.6 %all-reduce.18.cloned.1.call-start = ((), (), s32[]{:S(2)}) async-start(), calls=%async_computation.4 | async-start | bytes 17039360 | tf_op jit(solution)/shard_map/psum | solution.py:269
  388.1 42.8 %collective-permute-start.2 = (bf16[1024,256]{0,1:T(8,128)(2,1)}, bf16[1024,256]{0,1:T(8,128)(2,1)S(1)}, u32[]{:S(2)}, u32[]{:S(2)}) collective-permute-start(bf16[1024,256]{0,1:T(8,128)(2,1)} %get-tuple-element.110), channel_id=1, source_target_pairs={{4,0},{8,4},{12,8},{16,12},{20,16},{24,20},{28,24},{5,1},{9,5},{13... | collective-permute-start | bytes 1572872 | tf_op jit(solution)/shard_map/ppermute | solution.py:17
  389.4 41.6 %copy-start.33 = (bf16[1024,1024]{1,0:T(8,128)(2,1)S(1)}, bf16[1024,1024]{1,0:T(8,128)(2,1)}, u32[]{:S(2)}) copy-start(bf16[1024,1024]{1,0:T(8,128)(2,1)} %copy-done.32) | copy-start | bytes 6291460
  389.5 51.8 %collective-permute-start.3 = (bf16[1024,256]{0,1:T(8,128)(2,1)}, bf16[1024,256]{0,1:T(8,128)(2,1)S(1)}, u32[]{:S(2)}, u32[]{:S(2)}) collective-permute-start(bf16[1024,256]{0,1:T(8,128)(2,1)} %get-tuple-element.111), channel_id=1, source_target_pairs={{4,0},{8,4},{12,8},{16,12},{20,16},{24,20},{28,24},{5,1},{9,5},{13... | collective-permute-start | bytes 1572872 | tf_op jit(solution)/shard_map/ppermute | solution.py:17
  396.9 44.3 %copy-start.49 = (f32[4,64,1024]{2,1,0:T(8,128)S(1)}, f32[4,64,1024]{2,1,0:T(8,128)}, u32[]{:S(2)}) copy-start(f32[4,64,1024]{2,1,0:T(8,128)} %fusion.22) | copy-start | bytes 3145732
  444.1 407.0 %all-reduce.20.cloned.1.call-start = ((), (), s32[]{:S(2)}) async-start(), calls=%async_computation.5 | async-start | bytes 13107200 | tf_op jit(solution)/shard_map/psum | solution.py:83
  751.8 99.3 %copy-start.54 = (f32[1024]{0:T(1024)S(1)}, f32[1024]{0:T(1024)}, u32[]{:S(2)}) copy-start(f32[1024]{0:T(1024)} %copy-done.53) | copy-start | bytes 12292
  751.8 99.3 %copy-start.56 = (f32[1024]{0:T(1024)S(1)}, f32[1024]{0:T(1024)}, u32[]{:S(2)}) copy-start(f32[1024]{0:T(1024)} %copy-done.55) | copy-start | bytes 12292
  751.8 99.3 %copy-start.58 = (f32[1,1024]{1,0:T(1,128)S(1)}, f32[1,1024]{1,0:T(1,128)}, u32[]{:S(2)}) copy-start(f32[1,1024]{1,0:T(1,128)} %copy-done.57) | copy-start | bytes 12292
  751.8 103.0 %copy-start.64 = (f32[1024]{0:T(1024)S(1)}, f32[1024]{0:T(1024)}, u32[]{:S(2)}) copy-start(f32[1024]{0:T(1024)} %get-tuple-element.182) | copy-start | bytes 12292
  751.8 103.0 %copy-start.63 = (f32[1024]{0:T(1024)S(1)}, f32[1024]{0:T(1024)}, u32[]{:S(2)}) copy-start(f32[1024]{0:T(1024)} %get-tuple-element.173) | copy-start | bytes 12292
  751.8 103.1 %copy-start.66 = (bf16[3,256]{1,0:T(4,128)(2,1)S(1)}, bf16[3,256]{1,0:T(4,128)(2,1)}, u32[]{:S(2)}) copy-start(bf16[3,256]{1,0:T(4,128)(2,1)} %fusion.123) | copy-start | bytes 4612
  751.8 103.1 %copy-start.67 = (bf16[1,256]{1,0:T(2,128)(2,1)S(1)}, bf16[1,256]{1,0:T(2,128)(2,1)}, u32[]{:S(2)}) copy-start(bf16[1,256]{1,0:T(2,128)(2,1)} %stack.103) | copy-start | bytes 1540
  751.8 103.1 %copy-start.73 = (bf16[1024]{0:T(1024)(128)(2,1)S(1)}, bf16[1024]{0:T(1024)(128)(2,1)}, u32[]{:S(2)}) copy-start(bf16[1024]{0:T(1024)(128)(2,1)} %get-tuple-element.206) | copy-start | bytes 6148
  854.7 45.1 %copy-start.62 = (f32[1,1024]{1,0:T(1,128)S(1)}, f32[1,1024]{1,0:T(1,128)}, u32[]{:S(2)}) copy-start(f32[1,1024]{1,0:T(1,128)} %get-tuple-element.221) | copy-start | bytes 12292
  (66 other events, 296.9 us)
Sparse Core Ops, SparseCore 0:
  58.7 64.9 all-reduce.9
  143.3 51.4 all-reduce.11
  215.3 51.4 all-reduce.13
  287.9 51.4 all-reduce.15
  444.2 279.2 all-reduce.17
  728.1 122.9 all-reduce.19
where the time goes:
time: 924 us; the launch traced here: 914 us
  waiting for transfers between devices  599 us (65%)
  matrix products  130 us (14%)
  other arithmetic  81.6 us (9%)
  blocking collectives  37.5 us (4%)
  local copies, waits for them, and re-layouts  30.5 us (3%)
  between operations  17.6 us (2%)
  starting transfers between devices  13.6 us (1%)
    psum x1, waiting for transfers between devices, per_device(): lax.psum(text_key_part.astype(jnp.bfloat16), 'seq').astype(jnp.float32)  268 us
    psum x3, waiting for transfers between devices, tensor_rows(): lax.psum(partial_rows.astype(jnp.bfloat16), 'tensor').astype(jnp.float32)  207 us
    psum x2, waiting for transfers between devices, tensor_grads(): lax.psum(partial_rows.astype(jnp.bfloat16), 'tensor').astype(jnp.float32)  81.2 us
    ppermute x4, waiting for transfers between devices, shifted(): lax.ppermute(value, axis, [(source, source + steps) for source in range(l...  43.3 us
    psum x1, blocking collectives, per_device(): lax.psum(grad_gain.astype(jnp.bfloat16), 'seq').astype(jnp.float32)  37.5 us
    dot_general x10, matrix products, matmul_low(): return jnp.dot(left, right, preferred_element_type=jnp.float32)  26 us
    dot_general x10, matrix products, times_transpose(): jnp.einsum('ra,ba->rb', left, right, preferred_element_type=jnp.float32)  24.1 us
    dot_general x10, matrix products, contract_rows(): jnp.einsum('ra,rb->ab', left, right, preferred_element_type=jnp.float32)  21.6 us
  transfers between devices with their start and end apart: 10, of which 8 were waited for; matrix products, arithmetic and copies ran while one was open for 11% of the time, Pallas kernels for 0%

commit v1 on v0

v1 whole, which is shorter than its diff:
```python
import jax
import jax.numpy as jnp
from jax import lax
from jax.sharding import PartitionSpec as P

HEAD_SIZE = 64
ITEM_LEN = 1024


epsilon = 1e-05
masked_fill = -1e30


def shifted(value, axis, steps):
    count = lax.axis_size(axis)
    leading, last = (max(0, -steps), min(count, count - steps))
    return lax.ppermute(value, axis, [(source, source + steps) for source in range(leading, last)])


def matmul_low(left, right):
    return jnp.dot(left, right, preferred_element_type=jnp.float32)


def contract_rows(left, right):
    return jnp.einsum("ra,rb->ab", left, right, preferred_element_type=jnp.float32)


def times_transpose(left, right):
    return jnp.einsum("ra,ba->rb", left, right, preferred_element_type=jnp.float32)


def layer_norm(rows_in, gain, shift):
    row_mean = jnp.mean(rows_in, axis=-1, keepdims=True)
    centered = rows_in - row_mean
    variance = jnp.mean(centered * centered, axis=-1, keepdims=True)
    inv_scale = lax.rsqrt(variance + epsilon)
    normal = centered * inv_scale
    return (normal * gain + shift, normal, inv_scale)


def norm_back(grad_normed, normal, inv_scale, gain):
    grad_normal = grad_normed * gain
    grad_mean = jnp.mean(grad_normal, axis=-1, keepdims=True)
    proj_mean = jnp.mean(grad_normal * normal, axis=-1, keepdims=True)
    return inv_scale * (grad_normal - grad_mean - normal * proj_mean)


def split_heads(matrix, head_size):
    return matrix.reshape(matrix.shape[0], matrix.shape[1] // head_size, head_size)


def swapped(value, axis, distance):
    count = lax.axis_size(axis)
    return lax.ppermute(value, axis, [(source, source ^ distance) for source in range(count)])


def axis_bits(axis):
    return (lax.axis_size(axis) - 1).bit_length()


def gather_relative(block, axis):
    blocks = {0: block}
    for bit in reversed(range(axis_bits(axis))):
        blocks.update(
            {d ^ (1 << bit): swapped(held, axis, 1 << bit) for d, held in list(blocks.items())}
        )
    return [blocks[d] for d in range(len(blocks))]


def rank_bit(axis, bit):
    return (lax.axis_index(axis) >> bit) & 1


def shard_offset(axis, row_count):
    offset = 0
    for bit in range(axis_bits(axis)):
        offset = offset + rank_bit(axis, bit) * (row_count >> (bit + 1))
    return offset


def scatter_rows(partial_rows, axis):
    held = partial_rows
    for bit in range(axis_bits(axis)):
        half = held.shape[0] // 2
        mine = rank_bit(axis, bit)
        sent = lax.dynamic_slice_in_dim(held, (1 - mine) * half, half, 0)
        kept = lax.dynamic_slice_in_dim(held, mine * half, half, 0)
        arrived = swapped(sent, axis, 1 << bit)
        held = kept.astype(jnp.float32) + arrived.astype(jnp.float32)
        if bit + 1 < axis_bits(axis):
            held = held.astype(jnp.bfloat16)
    return held


def gather_rows(shard, axis):
    blocks = gather_relative(shard, axis)
    rows = shard.shape[0]
    total = rows * len(blocks)
    own = shard_offset(axis, total)
    full = jnp.zeros((total,) + shard.shape[1:], shard.dtype)
    for d, block in enumerate(blocks):
        start = own
        for bit in range(axis_bits(axis)):
            if (d >> bit) & 1:
                size = total >> (bit + 1)
                start = start + size * (1 - 2 * rank_bit(axis, bit))
        full = lax.dynamic_update_slice_in_dim(full, block, start, 0)
    return full


def scatter_columns(partial, axis):
    held = partial
    for bit in reversed(range(axis_bits(axis))):
        half = held.shape[1] // 2
        mine = rank_bit(axis, bit)
        sent = lax.dynamic_slice_in_dim(held, (1 - mine) * half, half, 1)
        kept = lax.dynamic_slice_in_dim(held, mine * half, half, 1)
        held = kept + swapped(sent, axis, 1 << bit)
    return held


def group_sum(values, axis, turn):
    count = lax.axis_size(axis)
    members = [(place + turn) % count for place in range(count)]
    return lax.psum(values, axis, axis_index_groups=[members])


def butterfly_sum(value, axis):
    for bit in range(axis_bits(axis)):
        value = value + swapped(value, axis, 1 << bit)
    return value


def per_device(
    tokens,
    item_ids,
    text_states,
    text_lengths,
    norm_gain,
    norm_shift,
    w_self,
    b_self,
    w_self_out,
    w_cross_q,
    w_cross_kv,
    b_cross,
    w_cross_out,
    w_up,
    b_up,
    w_down,
    out_bias,
    d_out,
):
    f32, bf16 = jnp.float32, jnp.bfloat16
    row_count = tokens.shape[0]
    assert row_count == ITEM_LEN
    local_width = w_self.shape[2]
    head_count = local_width // HEAD_SIZE
    score_scale = HEAD_SIZE ** (-0.5)
    seq_rank = lax.axis_index("seq")
    tensor_rank = lax.axis_index("tensor")
    shard_rows = row_count // lax.axis_size("tensor")
    shard_start = shard_offset("tensor", row_count)
    cut = jnp.sum((item_ids == 0).astype(jnp.int32))
    row_index = jnp.arange(row_count, dtype=jnp.int32)
    old_item = row_index < cut

    def own_rows(full_rows):
        return lax.dynamic_slice_in_dim(full_rows, shard_start, shard_rows, 0)

    def local_cols(full_rows):
        return lax.dynamic_slice_in_dim(full_rows, tensor_rank * local_width, local_width, axis=1)

    own_allowed = (row_index[None, :] <= row_index[:, None]) & (
        old_item[None, :] == old_item[:, None]
    )
    far_allowed = old_item[:, None] & ~old_item[None, :] & (seq_rank > 0)

    residual = tokens.astype(f32)
    gain_rows = norm_gain.astype(f32)
    shift_rows = norm_shift.astype(f32)
    bias_rows = out_bias.astype(f32)
    normed_one, normal_one, inv_one = layer_norm(residual, gain_rows[0], shift_rows[0])
    inputs_one = normed_one.astype(bf16)
    keys_local = matmul_low(inputs_one, w_self[1]).astype(bf16)
    values_local = (matmul_low(inputs_one, w_self[2]) + b_self[1].astype(f32)).astype(bf16)
    keys_far, values_far = shifted((keys_local, values_local), "seq", 1)
    queries = (matmul_low(inputs_one, w_self[0]) + b_self[0].astype(f32)).astype(bf16)
    all_self_out = jnp.concatenate(gather_relative(w_self_out, "tensor"), axis=0)
    all_cross_out = jnp.concatenate(gather_relative(w_cross_out, "tensor"), axis=0)
    all_cross_q = jnp.concatenate(gather_relative(w_cross_q, "tensor"), axis=1)
    query_heads = split_heads(queries, HEAD_SIZE)

    def scores_of(key_block, allowed):
        scores = score_scale * jnp.einsum(
            "qhd,khd->hqk",
            query_heads,
            split_heads(key_block, HEAD_SIZE),
            preferred_element_type=f32,
        )
        return jnp.where(allowed[None], scores, masked_fill)

    def attend_block(state_now, key_block, value_block, allowed):
        old_max, old_total, old_acc = state_now
        scores = scores_of(key_block, allowed)
        new_max = jnp.maximum(old_max, jnp.max(scores, axis=-1))
        weights = jnp.where(allowed[None], jnp.exp(scores - new_max[..., None]), 0.0)
        factor = jnp.exp(old_max - new_max)
        new_total = old_total * factor + jnp.sum(weights, axis=-1)
        update = jnp.einsum(
            "hqk,khd->hqd",
            weights.astype(bf16),
            split_heads(value_block, HEAD_SIZE),
            preferred_element_type=f32,
        )
        return (new_max, new_total, old_acc * factor[..., None] + update)

    start_max = jnp.full((head_count, row_count), masked_fill, f32)
    start_total = jnp.zeros((head_count, row_count), f32)
    start_acc = jnp.zeros((head_count, row_count, HEAD_SIZE), f32)
    attn_state = attend_block(
        (start_max, start_total, start_acc), keys_local, values_local, own_allowed
    )
    run_max, run_total, run_acc = attend_block(attn_state, keys_far, values_far, far_allowed)
    attn_heads = run_acc / run_total[..., None]
    log_total = run_max + jnp.log(run_total)
    attended = jnp.transpose(attn_heads, (1, 0, 2)).reshape(row_count, local_width).astype(bf16)
    all_attended = jnp.concatenate(gather_relative(attended, "tensor"), axis=1)
    after_self = residual + (matmul_low(all_attended, all_self_out) + bias_rows[0])

    normed_two, normal_two, inv_two = layer_norm(after_self, gain_rows[1], shift_rows[1])
    inputs_two = normed_two.astype(bf16)
    cross_queries = (matmul_low(inputs_two, w_cross_q) + b_cross[0].astype(f32)).astype(bf16)
    item_total, slot_count = text_states.shape[:2]
    slot_total = item_total * slot_count
    window_slots = 2 * slot_count
    text_flat = text_states.reshape(slot_total, text_states.shape[2])
    text_window = lax.dynamic_slice_in_dim(text_flat, seq_rank * slot_count, window_slots, 0)
    text_keys = matmul_low(text_window, w_cross_kv[0]).astype(bf16)
    text_values = (matmul_low(text_window, w_cross_kv[1]) + b_cross[1].astype(f32)).astype(bf16)
    window_index = jnp.arange(window_slots, dtype=jnp.int32)
    first_part = window_index < slot_count
    item_lengths = lax.dynamic_slice_in_dim(text_lengths, seq_rank, 2)
    slot_live = window_index % slot_count < jnp.where(first_part, item_lengths[0], item_lengths[1])
    cross_allowed = ((first_part[None, :] == old_item[:, None]) & slot_live[None, :])[None]
    cross_heads = split_heads(cross_queries, HEAD_SIZE)
    text_key_heads = split_heads(text_keys, HEAD_SIZE)
    text_value_heads = split_heads(text_values, HEAD_SIZE)
    cross_scores = score_scale * jnp.einsum(
        "qhd,shd->hqs", cross_heads, text_key_heads, preferred_element_type=f32
    )
    cross_filled = jnp.where(cross_allowed, cross_scores, masked_fill)
    cross_exp = jnp.exp(cross_filled - jnp.max(cross_filled, axis=-1, keepdims=True))
    cross_probs = cross_exp / jnp.sum(cross_exp, axis=-1, keepdims=True)
    cross_low = cross_probs.astype(bf16)
    cross_rows = jnp.einsum("hqs,shd->qhd", cross_low, text_value_heads, preferred_element_type=f32)
    cross_attended = cross_rows.reshape(row_count, local_width).astype(bf16)
    all_cross_attended = jnp.concatenate(gather_relative(cross_attended, "tensor"), axis=1)
    after_cross = after_self + (matmul_low(all_cross_attended, all_cross_out) + bias_rows[1])

    normed_three, normal_three, inv_three = layer_norm(after_cross, gain_rows[2], shift_rows[2])
    inputs_three = normed_three.astype(bf16)
    hidden_pre = matmul_low(inputs_three, w_up) + b_up.astype(f32)
    hidden_act, gelu_back = jax.vjp(jax.nn.gelu, hidden_pre)
    hidden_low = hidden_act.astype(bf16)
    grad_hidden = times_transpose(d_out, w_down)
    grad_pre = gelu_back(grad_hidden)[0].astype(bf16)
    grad_three_shard = scatter_rows(times_transpose(grad_pre, w_up).astype(bf16), "tensor")
    grad_w_down = contract_rows(hidden_low, d_out).astype(bf16)
    grad_w_up = contract_rows(inputs_three, grad_pre).astype(bf16)
    sum_w_down, sum_w_up = group_sum((grad_w_down, grad_w_up), "seq", 0)
    grad_b_up = jnp.sum(grad_pre.astype(f32), axis=0)
    output_shard = own_rows(after_cross) + (
        scatter_rows(matmul_low(hidden_low, w_down).astype(bf16), "tensor") + bias_rows[2]
    )
    output_rows = gather_rows(output_shard.astype(bf16), "tensor")

    normal_three_shard = own_rows(normal_three)
    grad_gain_three = jnp.sum(grad_three_shard * normal_three_shard, axis=0)
    grad_shift_three = jnp.sum(grad_three_shard, axis=0)
    grad_cross_shard = own_rows(d_out).astype(f32) + norm_back(
        grad_three_shard, normal_three_shard, own_rows(inv_three), gain_rows[2]
    )
    grad_cross_low = gather_rows(grad_cross_shard.astype(bf16), "tensor")
    grad_w_cross_out = contract_rows(cross_attended, grad_cross_low).astype(bf16)
    grad_cross_att = times_transpose(grad_cross_low, w_cross_out).astype(bf16)
    grad_cross_heads = split_heads(grad_cross_att, HEAD_SIZE)
    grad_cross_probs = jnp.einsum(
        "qhd,shd->hqs", grad_cross_heads, text_value_heads, preferred_element_type=f32
    )
    cross_inner = jnp.sum(cross_probs * grad_cross_probs, axis=-1, keepdims=True)
    grad_cross_scores = (cross_probs * (grad_cross_probs - cross_inner)).astype(bf16)
    grad_cross_q = (
        score_scale
        * jnp.einsum("hqs,shd->qhd", grad_cross_scores, text_key_heads, preferred_element_type=f32)
    )
    grad_cross_q = grad_cross_q.reshape(row_count, local_width).astype(bf16)
    all_grad_cross_q = jnp.concatenate(gather_relative(grad_cross_q, "tensor"), axis=1)
    key_window_part = score_scale * jnp.einsum(
        "hqs,qhd->shd", grad_cross_scores, cross_heads, preferred_element_type=f32
    )
    value_window_part = jnp.einsum(
        "hqs,qhd->shd", cross_low, grad_cross_heads, preferred_element_type=f32
    )
    grad_w_cross_q = contract_rows(inputs_two, grad_cross_q).astype(bf16)
    sum_w_cross_out, sum_w_cross_q = group_sum((grad_w_cross_out, grad_w_cross_q), "seq", 1)
    window_parts = jnp.stack((key_window_part, value_window_part)).astype(bf16)
    all_parts = lax.all_gather(window_parts.reshape(2, 2, slot_count, local_width), "seq")
    all_parts = all_parts.astype(f32)
    empty = jnp.zeros_like(all_parts[:1, :, 0])
    text_sums = jnp.concatenate((all_parts[:, :, 0], empty)) + jnp.concatenate(
        (empty, all_parts[:, :, 1])
    )
    text_sums = text_sums.astype(bf16)
    grad_text_keys = text_sums[:, 0].reshape(slot_total, local_width)
    grad_text_values = text_sums[:, 1].reshape(slot_total, local_width)
    grad_w_cross_kv = jnp.stack(
        (contract_rows(text_flat, grad_text_keys), contract_rows(text_flat, grad_text_values))
    )
    grad_text_part = times_transpose(grad_text_keys, w_cross_kv[0]) + times_transpose(
        grad_text_values, w_cross_kv[1]
    )
    grad_text_shard = scatter_rows(grad_text_part.astype(bf16), "tensor").astype(bf16)
    grad_text = gather_rows(grad_text_shard, "tensor").astype(f32).reshape(text_states.shape)
    grad_value_bias = jnp.sum(grad_text_values.astype(f32), axis=0)

    grad_normed_two = times_transpose(all_grad_cross_q, all_cross_q)
    grad_gain_two = jnp.sum(local_cols(grad_normed_two) * local_cols(normal_two), axis=0)
    grad_shift_two = jnp.sum(local_cols(grad_normed_two), axis=0)
    grad_after_self = grad_cross_low.astype(f32) + norm_back(
        grad_normed_two, normal_two, inv_two, gain_rows[1]
    )
    grad_self_low = grad_after_self.astype(bf16)
    grad_w_self_out = contract_rows(attended, grad_self_low).astype(bf16)
    grad_attn_rows = times_transpose(grad_self_low, w_self_out).astype(bf16)
    grad_attn_heads = split_heads(grad_attn_rows, HEAD_SIZE)
    row_inner = jnp.einsum("qhd,hqd->hq", grad_attn_heads.astype(f32), attn_heads)

    def back_block(key_block, value_block, allowed):
        attn_probs = jnp.exp(scores_of(key_block, allowed) - log_total[..., None])
        grad_probs = jnp.einsum(
            "qhd,khd->hqk",
            grad_attn_heads,
            split_heads(value_block, HEAD_SIZE),
            preferred_element_type=f32,
        )
        grad_scores = (attn_probs * (grad_probs - row_inner[..., None])).astype(bf16)
        grad_q_block = score_scale * jnp.einsum(
            "hqk,khd->qhd",
            grad_scores,
            split_heads(key_block, HEAD_SIZE),
            preferred_element_type=f32,
        )
        grad_key_block = score_scale * jnp.einsum(
            "hqk,qhd->khd", grad_scores, query_heads, preferred_element_type=f32
        )
        grad_value_block = jnp.einsum(
            "hqk,qhd->khd", attn_probs.astype(bf16), grad_attn_heads, preferred_element_type=f32
        )
        return tuple(
            part.reshape(row_count, local_width)
            for part in (grad_q_block, grad_key_block, grad_value_block)
        )

    grad_q_far, grad_keys_far, grad_values_far = back_block(keys_far, values_far, far_allowed)
    carry_keys, carry_values = shifted(
        (grad_keys_far.astype(bf16), grad_values_far.astype(bf16)), "seq", -1
    )
    grad_q_own, grad_keys_own, grad_values_own = back_block(keys_local, values_local, own_allowed)
    grad_queries = (grad_q_far + grad_q_own).astype(bf16)
    grad_keys = (grad_keys_own + carry_keys.astype(f32)).astype(bf16)
    grad_values = (grad_values_own + carry_values.astype(f32)).astype(bf16)
    grad_normed_one = (
        times_transpose(grad_queries, w_self[0])
        + times_transpose(grad_keys, w_self[1])
        + times_transpose(grad_values, w_self[2])
    )
    grad_one_shard = scatter_rows(grad_normed_one.astype(bf16), "tensor")
    grad_w_self = jnp.stack(
        (
            contract_rows(inputs_one, grad_queries),
            contract_rows(inputs_one, grad_keys),
            contract_rows(inputs_one, grad_values),
        )
    ).astype(bf16)
    sum_w_self, sum_w_self_out = group_sum((grad_w_self, grad_w_self_out), "seq", 2)
    normal_one_shard = own_rows(normal_one)
    grad_gain_one = jnp.sum(grad_one_shard * normal_one_shard, axis=0)
    grad_shift_one = jnp.sum(grad_one_shard, axis=0)
    grad_token_shard = own_rows(grad_after_self) + norm_back(
        grad_one_shard, normal_one_shard, own_rows(inv_one), gain_rows[0]
    )
    grad_tokens = gather_rows(grad_token_shard.astype(bf16), "tensor").astype(f32)

    shard_sums = scatter_columns(
        jnp.stack((grad_gain_one, grad_shift_one, grad_gain_three, grad_shift_three)), "tensor"
    )

    def token_sum(rows_in):
        return jnp.sum(rows_in.astype(f32), axis=0)

    vectors = jnp.stack(
        (
            grad_gain_two,
            grad_shift_two,
            token_sum(local_cols(grad_self_low)),
            token_sum(local_cols(grad_cross_low)),
            token_sum(local_cols(d_out)),
            token_sum(grad_cross_q),
            token_sum(grad_queries),
            token_sum(grad_values),
        )
    )
    vectors = jnp.concatenate((shard_sums, vectors, grad_b_up.reshape(-1, local_width)))
    vectors = butterfly_sum(vectors, "seq")
    grad_gain = jnp.stack((vectors[0], vectors[4], vectors[2]))
    grad_shift = jnp.stack((vectors[1], vectors[5], vectors[3]))
    grad_bias_out = vectors[6:9]
    grad_b_cross = jnp.stack((vectors[9], grad_value_bias))
    return (
        output_rows,
        grad_tokens,
        grad_text,
        grad_gain,
        grad_shift,
        sum_w_self.astype(f32),
        vectors[10:12],
        sum_w_self_out.astype(f32),
        sum_w_cross_q.astype(f32),
        grad_w_cross_kv,
        grad_b_cross,
        sum_w_cross_out.astype(f32),
        sum_w_up.astype(f32),
        vectors[12:].reshape(-1),
        sum_w_down.astype(f32),
        grad_bias_out,
    )


def solution(mesh):
    placed = (
        P("seq", None),
        P(),
        P(),
        P(),
        P(),
        P(),
        P(None, None, "tensor"),
        P(None, "tensor"),
        P("tensor", None),
        P(None, "tensor"),
        P(None, None, "tensor"),
        P(None, "tensor"),
        P("tensor", None),
        P(None, "tensor"),
        P("tensor"),
        P("tensor", None),
        P(),
        P("seq", None),
    )
    return jax.shard_map(
        per_device,
        mesh=mesh,
        in_specs=placed,
        out_specs=(
            P("seq", None),
            P("seq", None),
            P(),
            P(None, "tensor"),
            P(None, "tensor"),
            P(None, None, "tensor"),
            P(None, "tensor"),
            P("tensor", None),
            P(None, "tensor"),
            P(None, None, "tensor"),
            P(None, "tensor"),
            P("tensor", None),
            P(None, "tensor"),
            P("tensor"),
            P("tensor", None),
            P(None, "tensor"),
        ),
        check_vma=False,
    )
```

time: 924 us -> 679 us (0.73)
  waiting for transfers between devices: 599 us -> 282 us
  matrix products: 130 us -> 172 us
  blocking collectives: 37.5 us -> 0 us
  local copies, waits for them, and re-layouts: 30.5 us -> 64.1 us
  starting transfers between devices: 13.6 us -> 39 us
  other arithmetic: 81.6 us -> 99.4 us
    psum x6 -> x3, waiting for transfers between devices: 556 us -> 174 us  [group_sum(): return lax.psum(values, axis, axis_index_groups=[members])]
    ppermute x0 -> x43, waiting for transfers between devices: none -> 88.9 us  [swapped(): lax.ppermute(value, axis, [(source, source ^ distance) for source in rang...]
    psum x1 -> x0, blocking collectives: 37.5 us -> none  [per_device(): lax.psum(grad_gain.astype(jnp.bfloat16), 'seq').astype(jnp.float32)]
    dot_general x5 -> x10, matrix products: 38.8 us -> 76.1 us  [the longest x2 21.1 us: back_block(): jnp.einsum('qhd,khd->hqk', grad_attn_heads, split_heads(value_block, HEAD...]
    ppermute x0 -> x43, starting transfers between devices: none -> 27.9 us  [swapped(): lax.ppermute(value, axis, [(source, source ^ distance) for source in rang...]
    ppermute x4, waiting for transfers between devices: 43.3 us -> 18.4 us  [shifted(): lax.ppermute(value, axis, [(source, source + steps) for source in range(l...]
    reduce_sum x1 -> x2, other arithmetic: 3.66 us -> 17.8 us  [attend_block(): new_total = old_total * factor + jnp.sum(weights, axis=-1)]
    dynamic_update_slice x2 -> x12, local copies, waits for them, and re-layouts: 2.35 us -> 16.1 us  [gather_rows(): full = lax.dynamic_update_slice_in_dim(full, block, start, 0)]
  transfers between devices with their start and end apart: 10 -> 51, of which waited for: 8 -> 18; matrix products, arithmetic and copies ran while one was open for 11% -> 44% of each run, Pallas kernels for 0% -> 0%
where the time goes in v1:
time: 679 us; the launch traced here: 672 us
  waiting for transfers between devices  282 us (42%)
  matrix products  172 us (25%)
  other arithmetic  99.4 us (15%)
  local copies, waits for them, and re-layouts  64.1 us (9%)
  starting transfers between devices  39 us (6%)
  between operations  15.6 us (2%)
    psum x3, waiting for transfers between devices, group_sum(): return lax.psum(values, axis, axis_index_groups=[members])  174 us
    ppermute x43, waiting for transfers between devices, swapped(): lax.ppermute(value, axis, [(source, source ^ distance) for source in rang...  88.9 us
    dot_general x10, matrix products, matmul_low(): return jnp.dot(left, right, preferred_element_type=jnp.float32)  29.9 us
    unnamed x181, local copies, waits for them, and re-layouts  28.5 us
    ppermute x43, starting transfers between devices, swapped(): lax.ppermute(value, axis, [(source, source ^ distance) for source in rang...  27.9 us
    dot_general x10, matrix products, contract_rows(): jnp.einsum('ra,rb->ab', left, right, preferred_element_type=jnp.float32)  25 us
    dot_general x10, matrix products, times_transpose(): jnp.einsum('ra,ba->rb', left, right, preferred_element_type=jnp.float32)  23.1 us
    dot_general x2, matrix products, back_block(): jnp.einsum('qhd,khd->hqk', grad_attn_heads, split_heads(value_block, HEAD...  21.1 us
  transfers between devices with their start and end apart: 51, of which 18 were waited for; matrix products, arithmetic and copies ran while one was open for 44% of the time, Pallas kernels for 0%

profile of v1, /device:TPU:0, one launch (start us, length us, event | category | flops | bytes accessed | tf_op | source)
XLA Modules:
  0.0 672.4 jit_solution(16838539305450841992)
XLA Ops:
  41.5 8.9 %fusion.175 = (f32[4,1024]{1,0:T(4,128)S(1)}, f32[4,1024,1024]{1,2,0:T(8,128)}) fusion(bf16[1024,4,64]{0,2,1:T(8,128)(2,1)S(1)} %bitcast.239, bf16[1024,4,64]{0,2,1:T(8,128)(2,1)} %bitcast.7, pred[1024,1024]{0,1:T(8,128)(4,1)S(1)} %get-tuple-element.115), kind=kOutput, calls=%fused_computation.317 | convolution fusion | flops 549449728 | bytes 18890752 | tf_op jit(solution)/shard_map/qhd,khd->hqk/dot_general | solution.py:195
  50.5 8.6 %fusion.176 = (f32[4,1024]{1,0:T(4,128)S(1)}, f32[4,1024,1024]{1,2,0:T(8,128)}) fusion(bf16[1024,4,64]{0,2,1:T(8,128)(2,1)S(1)} %bitcast.240, bf16[1024,4,64]{0,2,1:T(8,128)(2,1)} %bitcast.13, pred[1024,1024]{0,1:T(8,128)(4,1)S(1)} %get-tuple-element.116), kind=kOutput, calls=%fused_computation.318 | convolution fusion | flops 549449728 | bytes 18890752 | tf_op jit(solution)/shard_map/qhd,khd->hqk/dot_general | solution.py:195
  59.1 9.0 %fusion.3 = f32[4,1024]{1,0:T(4,128)S(1)} fusion(f32[4,1024,1024]{1,2,0:T(8,128)} %get-tuple-element.122, f32[4,1024]{1,0:T(4,128)S(1)} %get-tuple-element.103, pred[1024,1024]{0,1:T(8,128)(4,1)} %copy-done.5), kind=kLoop, calls=%fused_computation.11 | loop fusion | flops 12578816 | bytes 17858560 | tf_op jit(solution)/shard_map/reduce_sum | solution.py:209
  68.1 8.8 %fusion.5 = f32[4,1024]{1,0:T(4,128)S(1)} fusion(f32[4,1024,1024]{1,2,0:T(8,128)} %get-tuple-element.124, f32[4,1024]{1,0:T(4,128)S(1)} %get-tuple-element.77, pred[1024,1024]{0,1:T(8,128)(4,1)S(1)} %get-tuple-element.116), kind=kLoop, calls=%fused_computation.13 | loop fusion | flops 12578816 | bytes 17858560 | tf_op jit(solution)/shard_map/reduce_sum | solution.py:209
  76.9 8.1 %fusion.15 = f32[4,1024,64]{1,2,0:T(8,128)S(1)} fusion(bf16[1024,4,64]{0,2,1:T(8,128)(2,1)} %bitcast.11, f32[4,1024,1024]{1,2,0:T(8,128)} %get-tuple-element.122, f32[4,1024]{1,0:T(4,128)S(1)} %get-tuple-element.103, pred[1024,1024]{0,1:T(8,128)(4,1)} %copy-done.5), kind=kOutput, calls=%fused_computation.20 | convolution fusion | flops 549453824 | bytes 19415040 | tf_op jit(solution)/shard_map/hqk,khd->hqd/dot_general | solution.py:210
  85.1 10.6 %fusion.109 = (bf16[1024,4,64]{0,2,1:T(8,128)(2,1)}, f32[4,1024,64]{1,2,0:T(8,128)}) fusion(f32[4,1024,64]{1,2,0:T(8,128)S(1)} %fusion.15, f32[1024,4]{0,1:T(4,128)S(1)} %get-tuple-element.93, f32[1024,4]{0,1:T(4,128)S(1)} %get-tuple-element.92, f32[1024,4]{0,1:T(4,128)S(1)} %get-tuple-element.102, bf16[1024,4,64]{0,2,1:T(8,128)(2,1)} %bitcast.15, ...), kind=kOutput, calls=%fused_computation.172 | convolution fusion | flops 550764544 | bytes 21037056 | tf_op jit(solution)/shard_map/hqk,khd->hqd/dot_general | solution.py:210
  100.0 9.4 %collective-permute-done.3 = bf16[1024,256]{0,1:T(8,128)(2,1)S(1)} collective-permute-done((bf16[1024,256]{0,1:T(8,128)(2,1)}, bf16[1024,256]{0,1:T(8,128)(2,1)S(1)}, u32[]{:S(2)}, u32[]{:S(2)}) %collective-permute-start.3) | collective-permute-done | bytes 524320 | tf_op jit(solution)/shard_map/ppermute | solution.py:54
  134.6 12.3 %collective-permute-done.9 = bf16[1024,256]{0,1:T(8,128)(2,1)S(1)} collective-permute-done((bf16[1024,256]{0,1:T(8,128)(2,1)}, bf16[1024,256]{0,1:T(8,128)(2,1)S(1)}, u32[]{:S(2)}, u32[]{:S(2)}) %collective-permute-start.9) | collective-permute-done | bytes 524320 | tf_op jit(solution)/shard_map/ppermute | solution.py:54
  148.9 6.1 fusion.179
  161.6 5.7 convert_reduce_fusion.1
  178.4 8.3 %collective-permute-done.28 = bf16[1024,256]{1,0:T(8,128)(2,1)} collective-permute-done((bf16[1024,256]{1,0:T(8,128)(2,1)}, bf16[1024,256]{1,0:T(8,128)(2,1)}, u32[]{:S(2)}, u32[]{:S(2)}) %collective-permute-start.28) | collective-permute-done | bytes 524320 | tf_op jit(solution)/shard_map/ppermute | solution.py:54
  195.6 7.4 %collective-permute-done.20 = bf16[256,1024]{0,1:T(8,128)(2,1)S(1)} collective-permute-done((bf16[256,1024]{0,1:T(8,128)(2,1)S(1)}, bf16[256,1024]{0,1:T(8,128)(2,1)S(1)}, u32[]{:S(2)}, u32[]{:S(2)}) %collective-permute-start.20) | collective-permute-done | bytes 524320 | tf_op jit(solution)/shard_map/ppermute | solution.py:54
  210.5 8.3 %collective-permute-done.22 = bf16[256,1024]{0,1:T(8,128)(2,1)S(1)} collective-permute-done((bf16[256,1024]{0,1:T(8,128)(2,1)S(1)}, bf16[256,1024]{0,1:T(8,128)(2,1)S(1)}, u32[]{:S(2)}, u32[]{:S(2)}) %collective-permute-start.22) | collective-permute-done | bytes 524320 | tf_op jit(solution)/shard_map/ppermute | solution.py:54
  251.3 6.0 collective-permute-done.17
  257.3 8.1 %multiply_reduce_fusion.4 = (f32[1024]{0:T(1024)S(1)}, f32[1024]{0:T(1024)S(1)}, f32[1024,1024]{0,1:T(8,128)}) fusion(f32[1024]{0:T(1024)S(1)} %bitcast.263, f32[1024,1024]{0,1:T(8,128)} %get-tuple-element.85, bf16[1024,256]{0,1:T(8,128)(2,1)} %collective-permute-done.26, bf16[1024,256]{0,1:T(8,128)(2,1)} %collective-permute-done.25, ...), kind=kOutput, calls=%fused_computation.60 | convolution fusion | flops 2168453120 | bytes 12595200 | tf_op jit(solution)/shard_map/ra,ba->rb/dot_general | solution.py:29
  265.5 8.1 %fusion.168 = (bf16[1024,1024]{0,1:T(8,128)(2,1)}, f32[1024,1024]{0,1:T(8,128)}) fusion(f32[1024,1024]{0,1:T(8,128)} %get-tuple-element.85, f32[1024]{0:T(1024)S(1)} %broadcast_multiply_fusion, f32[1024]{0:T(1024)S(1)} %broadcast_multiply_fusion.1, f32[1024,1024]{0,1:T(8,128)} %get-tuple-element.135, f32[1024]{0:T(1024)S(1)} %bitcast.264, ...), kind=kLoop, calls=%fused_computation.310 | loop fusion | flops 8388608 | bytes 16793600 | tf_op jit(solution)/shard_map/convert_element_type | solution.py:333
  279.8 9.4 %fusion.7 = f32[4,64,1024]{2,1,0:T(8,128)} fusion(bf16[1024,4,64]{0,2,1:T(8,128)(2,1)S(1)} %bitcast.244, f32[4,1024,1024]{1,2,0:T(8,128)} %get-tuple-element.122, f32[4,1024]{1,0:T(4,128)S(1)} %get-tuple-element.74), kind=kOutput, calls=%fused_computation.15 | convolution fusion | flops 545259520 | bytes 18366464 | tf_op jit(solution)/shard_map/hqk,qhd->khd/dot_general | solution.py:357
  289.3 7.9 %multiply_convert_fusion.1 = bf16[4,1024,1024]{1,2,0:T(8,128)(2,1)S(1)} fusion(f32[4,1024,1024]{1,2,0:T(8,128)} %get-tuple-element.124, bf16[1024,4,64]{0,2,1:T(8,128)(2,1)S(1)} %bitcast.245, bf16[1024,4,64]{0,2,1:T(8,128)(2,1)} %bitcast.15, f32[4,1024]{1,0:T(4,128)S(1)} %get-tuple-element.136, f32[4,1024]{1,0:T(4,128)S(1)} %get-tuple-element.74), kind=kOutput, calls=%fused_computation.3 | convolution fusion | flops 553648128 | bytes 26247168 | tf_op jit(solution)/shard_map/qhd,khd->hqk/dot_general | solution.py:341
  297.2 13.2 %multiply_convert_fusion = bf16[4,1024,1024]{1,2,0:T(8,128)(2,1)} fusion(f32[4,1024,1024]{1,2,0:T(8,128)} %get-tuple-element.122, bf16[1024,4,64]{0,2,1:T(8,128)(2,1)} %bitcast.246, bf16[1024,4,64]{0,2,1:T(8,128)(2,1)} %bitcast.11, f32[4,1024]{1,0:T(4,128)S(1)} %get-tuple-element.136, f32[4,1024]{1,0:T(4,128)S(1)} %get-tuple-element.74), kind=kOutput, calls=%fused_computation.1 | convolution fusion | flops 553648128 | bytes 26247168 | tf_op jit(solution)/shard_map/qhd,khd->hqk/dot_general | solution.py:341
  324.9 18.4 %collective-permute-done.31 = bf16[1024,256]{0,1:T(8,128)(2,1)S(1)} collective-permute-done((bf16[1024,256]{0,1:T(8,128)(2,1)S(1)}, bf16[1024,256]{0,1:T(8,128)(2,1)S(1)}, u32[]{:S(2)}, u32[]{:S(2)}) %collective-permute-start.31) | collective-permute-done | bytes 524320 | tf_op jit(solution)/shard_map/ppermute | solution.py:17
  406.8 123.7 %all-reduce.9.cloned.1.call-done = (bf16[1024,1024]{1,0:T(8,128)(2,1)}, bf16[1024,1024]{1,0:T(8,128)(2,1)}) async-done(((bf16[1024,1024]{1,0:T(8,128)(2,1)}, bf16[1024,1024]{1,0:T(8,128)(2,1)}), (bf16[1024,1024]{1,0:T(8,128)(2,1)}, bf16[1024,1024]{1,0:T(8,128)(2,1)})) %all-reduce.9.cloned.1.call-update) | async-done | bytes 4194320 | tf_op jit(solution)/shard_map/psum | solution.py:125
  559.8 7.2 %collective-permute-done.35 = bf16[256,1024]{0,1:T(8,128)(2,1)} collective-permute-done((bf16[256,1024]{0,1:T(8,128)(2,1)}, bf16[256,1024]{0,1:T(8,128)(2,1)}, u32[]{:S(2)}, u32[]{:S(2)}) %collective-permute-start.35) | collective-permute-done | bytes 524320 | tf_op jit(solution)/shard_map/ppermute | solution.py:54
  567.9 11.3 %collective-permute-done.38 = bf16[288,1024]{1,0:T(8,128)(2,1)S(1)} collective-permute-done((bf16[288,1024]{1,0:T(8,128)(2,1)S(1)}, bf16[288,1024]{1,0:T(8,128)(2,1)S(1)}, u32[]{:S(2)}, u32[]{:S(2)}) %collective-permute-start.38) | collective-permute-done | bytes 589856 | tf_op jit(solution)/shard_map/ppermute | solution.py:54
  586.0 50.8 %all-reduce.13.cloned.1.call-done = (bf16[3,1024,256]{2,1,0:T(8,128)(2,1)}, bf16[256,1024]{1,0:T(8,128)(2,1)}) async-done(((bf16[3,1024,256]{2,1,0:T(8,128)(2,1)}, bf16[256,1024]{1,0:T(8,128)(2,1)}), (bf16[3,1024,256]{2,1,0:T(8,128)(2,1)}, bf16[256,1024]{1,0:T(8,128)(2,1)})) %all-reduce.13.cloned.1.call-update) | async-done | bytes 2097168 | tf_op jit(solution)/shard_map/psum | solution.py:125
  (431 shorter events, 281.1 us)
Async XLA Ops:
  7.2 372.4 %all-reduce.11.cloned.1.call-start = ((), (), s32[]{:S(2)}) async-start(), calls=%async_computation.2 | async-start | bytes 2097152 | tf_op jit(solution)/shard_map/psum | solution.py:125
  7.2 92.2 %collective-permute-start.6 = (bf16[256,1024]{1,0:T(8,128)(2,1)}, bf16[256,1024]{1,0:T(8,128)(2,1)}, u32[]{:S(2)}, u32[]{:S(2)}) collective-permute-start(bf16[256,1024]{1,0:T(8,128)(2,1)} %param.26), channel_id=1, source_target_pairs={{0,2},{1,3},{2,0},{3,1},{4,6},{5,7},{6,4},{7,5},{8,10},{9,11},{10,... | collective-permute-start | bytes 1572872 | tf_op jit(solution)/shard_map/ppermute | solution.py:54
  10.3 102.7 %collective-permute-start.5 = (bf16[256,1024]{1,0:T(8,128)(2,1)}, bf16[256,1024]{1,0:T(8,128)(2,1)}, u32[]{:S(2)}, u32[]{:S(2)}) collective-permute-start(bf16[256,1024]{1,0:T(8,128)(2,1)} %param.26), channel_id=1, source_target_pairs={{0,1},{1,0},{2,3},{3,2},{4,5},{5,4},{6,7},{7,6},{8,9},{9,8},{10,11... | collective-permute-start | bytes 1572872 | tf_op jit(solution)/shard_map/ppermute | solution.py:54
  10.3 123.8 %collective-permute-start.12 = (bf16[256,1024]{1,0:T(8,128)(2,1)}, bf16[256,1024]{1,0:T(8,128)(2,1)}, u32[]{:S(2)}, u32[]{:S(2)}) collective-permute-start(bf16[256,1024]{1,0:T(8,128)(2,1)} %param.30), channel_id=1, source_target_pairs={{0,2},{1,3},{2,0},{3,1},{4,6},{5,7},{6,4},{7,5},{8,10},{9,11},{10,... | collective-permute-start | bytes 1572872 | tf_op jit(solution)/shard_map/ppermute | solution.py:54
  25.4 25.1 %collective-permute-start = (bf16[1024,256]{0,1:T(8,128)(2,1)}, bf16[1024,256]{0,1:T(8,128)(2,1)}, u32[]{:S(2)}, u32[]{:S(2)}) collective-permute-start(bf16[1024,256]{0,1:T(8,128)(2,1)} %convolution_convert_fusion.12), channel_id=1, source_target_pairs={{0,4},{4,8},{8,12},{12,16},{16,20},{20,24},{24,28},{1,5},{5,9},{9,... | collective-permute-start | bytes 1572872 | tf_op jit(solution)/shard_map/ppermute | solution.py:17
  31.6 53.4 %collective-permute-start.1 = (bf16[1024,256]{0,1:T(8,128)(2,1)}, bf16[1024,256]{0,1:T(8,128)(2,1)}, u32[]{:S(2)}, u32[]{:S(2)}) collective-permute-start(bf16[1024,256]{0,1:T(8,128)(2,1)} %fusion.91), channel_id=1, source_target_pairs={{0,4},{4,8},{8,12},{12,16},{16,20},{20,24},{24,28},{1,5},{5,9},{9,... | collective-permute-start | bytes 1572872 | tf_op jit(solution)/shard_map/ppermute | solution.py:17
  173.7 77.0 %collective-permute-start.27 = (bf16[1024,256]{1,0:T(8,128)(2,1)}, bf16[1024,256]{1,0:T(8,128)(2,1)}, u32[]{:S(2)}, u32[]{:S(2)}) collective-permute-start(bf16[1024,256]{1,0:T(8,128)(2,1)} %param.27), channel_id=1, source_target_pairs={{0,1},{1,0},{2,3},{3,2},{4,5},{5,4},{6,7},{7,6},{8,9},{9,8},{10,11... | collective-permute-start | bytes 1572872 | tf_op jit(solution)/shard_map/ppermute | solution.py:54
  186.7 70.5 %collective-permute-start.29 = (bf16[1024,256]{1,0:T(8,128)(2,1)}, bf16[1024,256]{1,0:T(8,128)(2,1)}, u32[]{:S(2)}, u32[]{:S(2)}) collective-permute-start(bf16[1024,256]{1,0:T(8,128)(2,1)} %collective-permute-done.28), channel_id=1, source_target_pairs={{0,1},{1,0},{2,3},{3,2},{4,5},{5,4},{6,7},{7,6},{8,9},{9,8},{10,11... | collective-permute-start | bytes 1572872 | tf_op jit(solution)/shard_map/ppermute | solution.py:54
  195.3 23.5 %collective-permute-start.14 = (bf16[512,1024]{0,1:T(8,128)(2,1)S(1)}, bf16[512,1024]{0,1:T(8,128)(2,1)S(1)}, u32[]{:S(2)}, u32[]{:S(2)}) collective-permute-start(bf16[512,1024]{0,1:T(8,128)(2,1)S(1)} %constant_dynamic-slice_fusion.12), channel_id=1, source_target_pairs={{0,1},{1,0},{2,3},{3,2},{4,5},{5,4},{6,7},{7,6},{8,9},{9,8},{10,11... | collective-permute-start | bytes 3145736 | tf_op jit(solution)/shard_map/ppermute | solution.py:54
  227.7 18.7 %collective-permute-start.25 = (bf16[1024,256]{0,1:T(8,128)(2,1)}, bf16[1024,256]{0,1:T(8,128)(2,1)}, u32[]{:S(2)}, u32[]{:S(2)}) collective-permute-start(bf16[1024,256]{0,1:T(8,128)(2,1)} %bitcast.42), channel_id=1, source_target_pairs={{0,2},{1,3},{2,0},{3,1},{4,6},{5,7},{6,4},{7,5},{8,10},{9,11},{10,... | collective-permute-start | bytes 1572872 | tf_op jit(solution)/shard_map/ppermute | solution.py:54
  233.5 163.2 %all-gather.2.cloned.1.call-start = ((), (), s32[]{:S(2)}) async-start(), calls=%async_computation | async-start | bytes 2359296 | tf_op jit(solution)/shard_map/all_gather | solution.py:308
  250.7 279.8 %all-reduce.9.cloned.1.call-start = ((), (), s32[]{:S(2)}) async-start(), calls=%async_computation.1 | async-start | bytes 8388608 | tf_op jit(solution)/shard_map/psum | solution.py:125
  250.7 102.7 %collective-permute-start.16 = (bf16[256,1024]{0,1:T(8,128)(2,1)}, bf16[256,1024]{0,1:T(8,128)(2,1)}, u32[]{:S(2)}, u32[]{:S(2)}) collective-permute-start(bf16[256,1024]{0,1:T(8,128)(2,1)} %get-tuple-element.83), channel_id=1, source_target_pairs={{0,1},{1,0},{2,3},{3,2},{4,5},{5,4},{6,7},{7,6},{8,9},{9,8},{10,11... | collective-permute-start | bytes 1572872 | tf_op jit(solution)/shard_map/ppermute | solution.py:54
  257.2 100.0 %collective-permute-start.18 = (bf16[256,1024]{0,1:T(8,128)(2,1)}, bf16[256,1024]{0,1:T(8,128)(2,1)}, u32[]{:S(2)}, u32[]{:S(2)}) collective-permute-start(bf16[256,1024]{0,1:T(8,128)(2,1)} %collective-permute-done.17), channel_id=1, source_target_pairs={{0,1},{1,0},{2,3},{3,2},{4,5},{5,4},{6,7},{7,6},{8,9},{9,8},{10,11... | collective-permute-start | bytes 1572872 | tf_op jit(solution)/shard_map/ppermute | solution.py:54
  313.1 31.1 %collective-permute-start.30 = (bf16[1024,256]{0,1:T(8,128)(2,1)S(1)}, bf16[1024,256]{0,1:T(8,128)(2,1)S(1)}, u32[]{:S(2)}, u32[]{:S(2)}) collective-permute-start(bf16[1024,256]{0,1:T(8,128)(2,1)S(1)} %bitcast.254), channel_id=1, source_target_pairs={{4,0},{8,4},{12,8},{16,12},{20,16},{24,20},{28,24},{5,1},{9,5},{13... | collective-permute-start | bytes 1572872 | tf_op jit(solution)/shard_map/ppermute | solution.py:17
  314.4 29.0 %collective-permute-start.31 = (bf16[1024,256]{0,1:T(8,128)(2,1)S(1)}, bf16[1024,256]{0,1:T(8,128)(2,1)S(1)}, u32[]{:S(2)}, u32[]{:S(2)}) collective-permute-start(bf16[1024,256]{0,1:T(8,128)(2,1)S(1)} %bitcast.253), channel_id=1, source_target_pairs={{4,0},{8,4},{12,8},{16,12},{20,16},{24,20},{28,24},{5,1},{9,5},{13... | collective-permute-start | bytes 1572872 | tf_op jit(solution)/shard_map/ppermute | solution.py:17
  347.3 26.7 %collective-permute-start.32 = (bf16[512,1024]{0,1:T(8,128)(2,1)S(1)}, bf16[512,1024]{0,1:T(8,128)(2,1)}, u32[]{:S(2)}, u32[]{:S(2)}) collective-permute-start(bf16[512,1024]{0,1:T(8,128)(2,1)S(1)} %constant_dynamic-slice_fusion.7), channel_id=1, source_target_pairs={{0,1},{1,0},{2,3},{3,2},{4,5},{5,4},{6,7},{7,6},{8,9},{9,8},{10,11... | collective-permute-start | bytes 3145736 | tf_op jit(solution)/shard_map/ppermute | solution.py:54
  353.4 283.4 %all-reduce.13.cloned.1.call-start = ((), (), s32[]{:S(2)}) async-start(), calls=%async_computation.3 | async-start | bytes 4194304 | tf_op jit(solution)/shard_map/psum | solution.py:125
  396.6 140.5 %collective-permute-start.43 = (f32[4,256]{1,0:T(4,128)S(1)}, f32[4,256]{1,0:T(4,128)S(1)}, u32[]{:S(2)}, u32[]{:S(2)}) collective-permute-start(f32[4,256]{1,0:T(4,128)S(1)} %constant_dynamic-slice_fusion), channel_id=1, source_target_pairs={{0,1},{1,0},{2,3},{3,2},{4,5},{5,4},{6,7},{7,6},{8,9},{9,8},{10,11... | collective-permute-start | bytes 12296 | tf_op jit(solution)/shard_map/ppermute | solution.py:54
  404.9 148.5 %collective-permute-start.37 = (bf16[576,1024]{1,0:T(8,128)(2,1)}, bf16[576,1024]{1,0:T(8,128)(2,1)}, u32[]{:S(2)}, u32[]{:S(2)}) collective-permute-start(bf16[576,1024]{1,0:T(8,128)(2,1)} %constant_dynamic-slice_fusion.5), channel_id=1, source_target_pairs={{0,1},{1,0},{2,3},{3,2},{4,5},{5,4},{6,7},{7,6},{8,9},{9,8},{10,11... | collective-permute-start | bytes 3538952 | tf_op jit(solution)/shard_map/ppermute | solution.py:54
  552.0 93.3 %collective-permute-start.34 = (bf16[256,1024]{0,1:T(8,128)(2,1)}, bf16[256,1024]{0,1:T(8,128)(2,1)}, u32[]{:S(2)}, u32[]{:S(2)}) collective-permute-start(bf16[256,1024]{0,1:T(8,128)(2,1)} %get-tuple-element.73), channel_id=1, source_target_pairs={{0,1},{1,0},{2,3},{3,2},{4,5},{5,4},{6,7},{7,6},{8,9},{9,8},{10,11... | collective-permute-start | bytes 1572872 | tf_op jit(solution)/shard_map/ppermute | solution.py:54
  555.3 23.8 %collective-permute-start.38 = (bf16[288,1024]{1,0:T(8,128)(2,1)S(1)}, bf16[288,1024]{1,0:T(8,128)(2,1)S(1)}, u32[]{:S(2)}, u32[]{:S(2)}) collective-permute-start(bf16[288,1024]{1,0:T(8,128)(2,1)S(1)} %constant_dynamic-slice_fusion.4), channel_id=1, source_target_pairs={{0,2},{1,3},{2,0},{3,1},{4,6},{5,7},{6,4},{7,5},{8,10},{9,11},{10,... | collective-permute-start | bytes 1769480 | tf_op jit(solution)/shard_map/ppermute | solution.py:54
  567.0 83.3 %collective-permute-start.36 = (bf16[256,1024]{0,1:T(8,128)(2,1)}, bf16[256,1024]{0,1:T(8,128)(2,1)}, u32[]{:S(2)}, u32[]{:S(2)}) collective-permute-start(bf16[256,1024]{0,1:T(8,128)(2,1)} %collective-permute-done.35), channel_id=1, source_target_pairs={{0,1},{1,0},{2,3},{3,2},{4,5},{5,4},{6,7},{7,6},{8,9},{9,8},{10,11... | collective-permute-start | bytes 1572872 | tf_op jit(solution)/shard_map/ppermute | solution.py:54
  582.2 65.1 %collective-permute-start.40 = (bf16[288,1024]{1,0:T(8,128)(2,1)}, bf16[288,1024]{1,0:T(8,128)(2,1)}, u32[]{:S(2)}, u32[]{:S(2)}) collective-permute-start(bf16[288,1024]{1,0:T(8,128)(2,1)} %get-tuple-element.71), channel_id=1, source_target_pairs={{0,2},{1,3},{2,0},{3,1},{4,6},{5,7},{6,4},{7,5},{8,10},{9,11},{10,... | collective-permute-start | bytes 1769480 | tf_op jit(solution)/shard_map/ppermute | solution.py:54
  (114 other events, 1058.2 us)
Sparse Core Ops, SparseCore 0:
  233.6 77.6 all-reduce.10
  313.7 54.8 all-gather.1
  372.8 157.5 all-reduce.8
  535.0 101.7 all-reduce.12
